TPU v7x, 256 devices: a whole 4x4x8 slice. The times are simulated.
256 devices in a mesh: dp: 4 (over x), ctx: 16 (over z, core), tp: 4 (over y).
Axes of the slice: x: 4, y: 4, z: 8, core: 2. Of those that a mesh axis runs over, the one named last changes fastest.
Arguments:
- queries: bfloat16 [16384, 8192], P(('dp', 'ctx'), 'tp'), parts along dimension 0, may hold values from -50 to 50
- key_value_vectors: bfloat16 [16384, 2048], P(('dp', 'ctx'), 'tp'), parts along dimension 0, may hold values from -12 to 12
- out_weight: bfloat16 [8192, 4096], P('tp', 'ctx'), may hold values from -0.5 to 0.5
- doc_lengths: int32 [32], P('dp'), parts along dimension 0, may hold values from 1 to 1024, 4096 in all
- shard_of: int32 [16384], P(('dp', 'ctx')), parts along dimension 0, may hold values from 0 to 15, as said below
Outputs:
- output: bfloat16 [16384, 4096], P(('dp', 'ctx'), 'tp'), parts along dimension 0
There are 4 independent parts, one for each index of `dp`. A program takes and returns all parts, laid end to end along the dimension named above; an argument that names none is the same for every part. Nothing has to cross between parts.
Inputs may be any that keep to these rules, and one draw needn't show every extreme that they name: `shard_of`: every aligned block of 16 positions has one shard; each shard holds exactly 256 tokens; the tokens of one context shard's input rows go to 8 shards, exactly 32 tokens to each.
All inputs are finite; a program needn't handle non-finite values.
Results may differ from a plain program's by a relative error of at most 0.0053.
Values may be sent and summed in bfloat16 or wider, within the bound.
A program may use at most 128 MiB of HBM per device.

v0:
```python
import math

import jax
import jax.numpy as jnp
from jax import lax
from jax.sharding import PartitionSpec as P

HEAD_SIZE = 128


def block_count():
    block_total = 1
    for attempt in range(3):
        block_total = block_total * 2
    return block_total


def attend(queries_all, pairs_all, query_pos, query_doc, key_pos, key_doc):
    row_count = queries_all.shape[0]
    head_count = queries_all.shape[1]
    groups = pairs_all.shape[1]
    group_ratio = head_count // groups
    pieces = block_count()
    span_rows = row_count // pieces
    keys_all = pairs_all[:, :, :HEAD_SIZE]
    values_all = pairs_all[:, :, HEAD_SIZE:]
    score_scale = 1.0 / math.sqrt(HEAD_SIZE)
    results = []
    for number in range(pieces):
        row_start = number * span_rows
        key_limit = row_start + span_rows
        block_q = queries_all[row_start : row_start + span_rows].reshape(
            span_rows, groups, group_ratio, HEAD_SIZE
        )
        scores = (
            jnp.einsum(
                "qgrd,kgd->grqk", block_q, keys_all[:key_limit], preferred_element_type=jnp.float32
            )
            * score_scale
        )
        allowed = (
            key_doc[None, :key_limit] == query_doc[row_start : row_start + span_rows, None]
        ) & (key_pos[None, :key_limit] <= query_pos[row_start : row_start + span_rows, None])
        scores = jnp.where(allowed[None, None], scores, -1e30)
        row_peak = jnp.max(scores, axis=3, keepdims=True)
        weights = jnp.exp(scores - row_peak)
        totals = jnp.sum(weights, axis=3)
        mixed_out = jnp.einsum(
            "grqk,kgd->qgrd",
            weights.astype(jnp.bfloat16),
            values_all[:key_limit],
            preferred_element_type=jnp.float32,
        )
        mixed_out = mixed_out / jnp.transpose(totals, (2, 0, 1))[:, :, :, None]
        results.append(mixed_out.reshape(span_rows, head_count, HEAD_SIZE).astype(jnp.bfloat16))
    return jnp.concatenate(results, axis=0)


def local(queries, key_value_vectors, out_weight, doc_lengths, shard_of):
    ctx_count = lax.axis_size("ctx")
    tok_rows = queries.shape[0]
    all_rows = tok_rows * ctx_count
    local_heads = queries.shape[1] // HEAD_SIZE
    local_groups = key_value_vectors.shape[1] // (2 * HEAD_SIZE)
    group_size = local_heads // local_groups
    owners = lax.all_gather(shard_of, "ctx", axis=0, tiled=True)
    positions = jnp.arange(all_rows, dtype=jnp.int32)
    doc_ends = jnp.cumsum(doc_lengths)
    doc_of = jnp.sum((positions[:, None] >= doc_ends[None, :]).astype(jnp.int32), axis=1)
    shard_ids = jnp.arange(ctx_count, dtype=jnp.int32)
    owner_hot = (owners[:, None] == shard_ids[None, :]).astype(jnp.int32)
    rank_in = jnp.sum((jnp.cumsum(owner_hot, axis=0) - owner_hot) * owner_hot, axis=1)
    packed_index = owners * tok_rows + rank_in
    packed_pos = jnp.zeros((all_rows,), jnp.int32).at[packed_index].set(positions)
    query_three = queries.reshape(tok_rows, local_heads, HEAD_SIZE)
    pair_three = key_value_vectors.reshape(tok_rows, local_groups, 2 * HEAD_SIZE)
    head_query = lax.all_to_all(query_three, "ctx", split_axis=1, concat_axis=0, tiled=True)
    head_pairs = lax.all_to_all(
        jnp.repeat(pair_three, group_size, axis=1), "ctx", split_axis=1, concat_axis=0, tiled=True
    )
    attended = attend(head_query, head_pairs, positions, doc_of, positions, doc_of)
    hidden = lax.all_to_all(attended[packed_pos], "ctx", split_axis=0, concat_axis=1, tiled=True)
    hidden_rows = hidden.reshape(tok_rows, local_heads * HEAD_SIZE)
    partial_terms = jnp.dot(
        hidden_rows,
        lax.all_gather(out_weight, "ctx", axis=1, tiled=True),
        preferred_element_type=jnp.float32,
    )
    summed = lax.psum_scatter(partial_terms, "tp", scatter_dimension=1, tiled=True)
    return summed.astype(jnp.bfloat16)


def solution(mesh):
    placed = (
        P(("dp", "ctx"), "tp"),
        P(("dp", "ctx"), "tp"),
        P("tp", "ctx"),
        P("dp"),
        P(("dp", "ctx")),
    )
    return jax.shard_map(
        local, mesh=mesh, in_specs=placed, out_specs=P(("dp", "ctx"), "tp"), check_vma=False
    )
```

profile of v0, /device:TPU:1, one launch (start us, length us, event | category | flops | bytes accessed | tf_op | source)
XLA Modules:
  0.0 321.7 jit_solution(4027595356701155466)
XLA Ops:
  7.3 2.3 copy.43
  9.5 10.1 %all-to-all-start.1 = ((bf16[256,16,128]{0,2,1:T(8,128)(2,1)}), bf16[256,16,128]{0,2,1:T(8,128)(2,1)S(1)}, u32[]{:S(2)}, u32[]{:S(2)}) async-start(bf16[256,16,128]{0,2,1:T(8,128)(2,1)} %bitcast.7), calls=%async_computation.1 | async-start | bytes 2097152 | tf_op jit(solution)/shard_map/all_to_all | solution.py:77
  19.7 36.6 %all-to-all-done.1 = bf16[256,16,128]{0,2,1:T(8,128)(2,1)S(1)} async-done(((bf16[256,16,128]{0,2,1:T(8,128)(2,1)}), bf16[256,16,128]{0,2,1:T(8,128)(2,1)S(1)}, u32[]{:S(2)}, u32[]{:S(2)}) %all-to-all-start.1) | async-done | bytes 1048608 | tf_op jit(solution)/shard_map/all_to_all | solution.py:77
  56.3 1.6 broadcast_in_dim.33
  57.9 5.0 %all-to-all-start = ((bf16[256,16,256]{2,0,1:T(8,128)(2,1)}), bf16[256,16,256]{2,0,1:T(8,128)(2,1)S(1)}, u32[]{:S(2)}, u32[]{:S(2)}) async-start(bf16[256,16,256]{2,0,1:T(8,128)(2,1)} %bitcast.407), calls=%async_computation | async-start | bytes 4194304 | tf_op jit(solution)/shard_map/all_to_all | solution.py:78
  63.8 74.3 %all-gather = s32[16,1,256]{2,1,0:T(1,128)S(1)} all-gather(s32[1,1,256]{2,1,0:T(1,128)S(1)} %bitcast.428), channel_id=1, replica_groups=mesh['dp'=4,'ctx'=16,'tp'=4] {'ctx'}, dimensions={0}, use_global_device_ids=true | all-gather | bytes 17408 | tf_op jit(solution)/shard_map/all_gather | solution.py:66
  138.8 8.3 %reduce-window.19 = s32[16,32,128]{2,1,0:T(8,128)S(1)} reduce-window(s32[16,32,128]{2,1,0:T(8,128)} %fusion.151, s32[]{:T(128)} %constant.7.clone.1), window={size=1x1x128 pad=0_0x0_0x127_0}, to_apply=%region_18.19 | reduce-window | flops 8323072 | bytes 524292 | tf_op jit(solution)/shard_map/reduce-window.1
  148.1 15.7 %scatter_custom_fusion = s32[4096]{0:T(1024)S(1)} fusion(s32[4096]{0:T(1024)S(1)} %compare_select_fusion.1, s32[4096]{0:T(1024)S(1)} %iota.44, s32[]{:T(128)} %constant.7.clone.1), kind=kCustom, calls=%fused_computation.138 | custom fusion | bytes 16388 | tf_op jit(solution)/shard_map/scatter | solution.py:74
  176.7 1.7 copy.47
  178.4 1.6 copy.48
  182.5 1.3 fusion.158
  189.1 1.3 fusion.161
  192.1 1.6 fusion.162
  195.9 1.8 fusion.163
  199.9 2.0 fusion.164
  201.9 1.2 fusion.1
  203.1 1.3 fusion.129
  204.4 1.4 fusion.99
  205.8 12.1 %gather_fusion = bf16[4096,128]{1,0:T(8,128)(2,1)S(1)} fusion(bf16[4096,128]{1,0:T(8,128)(2,1)S(1)} %bitcast.390, s32[4096]{0:T(1024)S(1)} %copy-done.6), kind=kCustom, calls=%fused_computation | custom fusion | bytes 2113536 | tf_op jit(solution)/shard_map/gather | solution.py:82
  218.5 1.4 reduce.18
  220.2 34.3 %all_to_all.48 = bf16[16,2,16384]{2,1,0:T(2,128)(2,1)S(1)} all-to-all(bf16[16,2,16384]{2,1,0:T(2,128)(2,1)S(1)} %reshape.1167), channel_id=1, replica_groups=mesh['dp'=4,'ctx'=16,'tp'=4] {'ctx'}, dimensions={0} | all-to-all | bytes 2097152 | tf_op jit(solution)/shard_map/all_to_all | solution.py:82
  256.3 10.1 %fusion.165 = f32[256,4096]{1,0:T(8,128)} fusion(bf16[256,2048]{0,1:T(8,128)(2,1)S(1)} %bitcast.408, bf16[2048,4096]{1,0:T(8,128)(2,1)} %all-gather.3.cloned.1.call-done), kind=kOutput, calls=%fused_computation.159 | convolution fusion | flops 4294967296 | bytes 22020096 | tf_op jit(solution)/shard_map/dot_general | solution.py:84
  266.4 46.3 %reduce-scatter.2.cloned.1.call-done = f32[256,1024]{1,0:T(8,128)} async-done(((f32[256,4096]{1,0:T(8,128)}), f32[256,1024]{1,0:T(8,128)}) %reduce-scatter.2.cloned.1.call-update) | async-done | bytes 1048592 | tf_op jit(solution)/shard_map/reduce_scatter | solution.py:89
  312.7 2.1 convert_element_type.208
  (126 shorter events, 32.2 us)
Async XLA Ops:
  6.5 13.1 %copy-start.2 = (bf16[256,512]{1,0:T(8,128)(2,1)S(1)}, bf16[256,512]{1,0:T(8,128)(2,1)}, u32[]{:S(2)}) copy-start(bf16[256,512]{1,0:T(8,128)(2,1)} %param.6) | copy-start | bytes 786436
  6.5 249.7 %all-gather.3.cloned.1.call-start = ((), (), s32[]{:S(2)}) async-start(), calls=%async_computation.4 | async-start | bytes 17825792 | tf_op jit(solution)/shard_map/all_gather | solution.py:86
  9.5 53.3 %copy-start.28 = (s32[8]{0:T(128)S(1)}, s32[8]{0:T(128)}, u32[]{:S(2)}) copy-start(s32[8]{0:T(128)} %param.8) | copy-start | bytes 100
  9.5 54.2 %copy-start.27 = (s32[256]{0:T(256)S(1)}, s32[256]{0:T(256)}, u32[]{:S(2)}) copy-start(s32[256]{0:T(256)} %param.9) | copy-start | bytes 3076
  9.5 46.8 %all-to-all-start.1 = ((bf16[256,16,128]{0,2,1:T(8,128)(2,1)}), bf16[256,16,128]{0,2,1:T(8,128)(2,1)S(1)}, u32[]{:S(2)}, u32[]{:S(2)}) async-start(bf16[256,16,128]{0,2,1:T(8,128)(2,1)} %bitcast.7), calls=%async_computation.1 | async-start | bytes 2097152 | tf_op jit(solution)/shard_map/all_to_all | solution.py:77
  57.9 123.2 %all-to-all-start = ((bf16[256,16,256]{2,0,1:T(8,128)(2,1)}), bf16[256,16,256]{2,0,1:T(8,128)(2,1)S(1)}, u32[]{:S(2)}, u32[]{:S(2)}) async-start(bf16[256,16,256]{2,0,1:T(8,128)(2,1)} %bitcast.407), calls=%async_computation | async-start | bytes 4194304 | tf_op jit(solution)/shard_map/all_to_all | solution.py:78
  62.8 249.9 %reduce-scatter.2.cloned.1.call-start = ((), (), s32[]{:S(2)}) async-start(), calls=%async_computation.5 | async-start | bytes 5242880 | tf_op jit(solution)/shard_map/reduce_scatter | solution.py:89
  63.2 119.1 %copy-start = (s32[4096]{0:T(1024)}, s32[4096]{0:T(1024)S(1)}, u32[]{:S(2)}) copy-start(s32[4096]{0:T(1024)S(1)} %convert_reduce_fusion) | copy-start | bytes 49156
  173.6 8.9 %copy-start.12 = (s32[1024]{0:T(1024)S(1)}, s32[1024]{0:T(1024)}, u32[]{:S(2)}) copy-start(s32[1024]{0:T(1024)} %iota_add_fusion.5) | copy-start | bytes 12292
  173.6 8.9 %copy-start.19 = (s32[512]{0:T(512)S(1)}, s32[512]{0:T(512)}, u32[]{:S(2)}) copy-start(s32[512]{0:T(512)} %get-tuple-element.19) | copy-start | bytes 6148
  173.6 8.9 %copy-start.26 = (s32[512]{0:T(512)S(1)}, s32[512]{0:T(512)}, u32[]{:S(2)}) copy-start(s32[512]{0:T(512)} %iota_add_fusion.12) | copy-start | bytes 6148
  181.1 3.1 copy-start.11
  181.1 3.1 copy-start.18
  181.1 3.1 copy-start.25
  182.3 1.9 slice-start
  185.0 1.5 slice-start.1
  185.0 1.5 copy-start.5
  185.1 1.5 copy-start.10
  185.1 1.5 copy-start.17
  190.4 1.6 slice-start.3
  190.4 1.6 copy-start.3
  190.5 1.6 copy-start.8
  190.5 1.6 copy-start.15
  190.5 1.6 copy-start.22
  (13 other events, 16.2 us)
Sparse Core Ops, SparseCore 0:
  9.1 170.5 all-gather.2
  266.5 46.1 reduce-scatter.1
where the time goes:
time: 323 us; the launch traced here: 322 us
  blocking collectives  109 us (34%)
  waiting for transfers between devices  83.7 us (26%)
  local copies, waits for them, and re-layouts  43.7 us (14%)
  matrix products  28.5 us (9%)
  other arithmetic  28.1 us (9%)
  starting transfers between devices  15.1 us (5%)
  between operations  14 us (4%)
    all_gather x1, blocking collectives, local(): owners = lax.all_gather(shard_of, 'ctx', axis=0, tiled=True)  74.3 us
    reduce_scatter x1, waiting for transfers between devices, local(): lax.psum_scatter(partial_terms, 'tp', scatter_dimension=1, tiled=True)  46.3 us
    all_to_all x1, waiting for transfers between devices, local(): lax.all_to_all(query_three, 'ctx', split_axis=1, concat_axis=0, tiled=True)  36.6 us
    all_to_all x1, blocking collectives, local(): lax.all_to_all(attended[packed_pos], 'ctx', split_axis=0, concat_axis=1,...  34.3 us
    scatter x1, local copies, waits for them, and re-layouts, local(): jnp.zeros((all_rows,), jnp.int32).at[packed_index].set(positions)  15.7 us
    gather x2, local copies, waits for them, and re-layouts, local(): attended[packed_pos]  12.6 us
    dot_general x8, matrix products, attend(): jnp.einsum('qgrd,kgd->grqk', block_q, keys_all[:key_limit], preferred_ele...  11.1 us
    all_to_all x1, starting transfers between devices, local(): lax.all_to_all(query_three, 'ctx', split_axis=1, concat_axis=0, tiled=True)  10.1 us
  transfers between devices with their start and end apart: 4, of which 2 were waited for; matrix products, arithmetic and copies ran while one was open for 27% of the time, Pallas kernels for 0%

commit v1 on v0

v1 whole, which is shorter than its diff:
```python
import math

import jax
import jax.numpy as jnp
from jax import lax
from jax.experimental import pallas as pl
from jax.experimental.pallas import tpu as pltpu
from jax.sharding import PartitionSpec as P

MESH = pl.DeviceIdType.MESH
BF = jnp.bfloat16
F32 = jnp.float32
HS = 128
TOK = 256
GH = 8
GW = GH * HS
NK = 5 * TOK
SCALE = math.log2(math.e) / math.sqrt(HS)
NZ = 8
NC = 16
NT = 4


def mult(value, of):
    return pl.multiple_of(value, of)


def kernel(
    q_ref, kv_ref, w_ref, meta_ref, len_ref, out_ref,
    qbuf, kvb, vo, bias, hbuf, wbuf, pbuf, rbuf, red, sbuf, gbuf, sel, take, mbuf, msm,
    loc, m_s, m_r, q_s, q_r, kv_s, kv_r, w_s, w_r, h_s, h_r, y_s, y_r, g_s, g_r,
):
    x = lax.axis_index("dp")
    c = lax.axis_index("ctx")
    t = lax.axis_index("tp")
    z = c // 2
    k = lax.rem(c, 2)
    xp = lax.rem(x, 2)
    xq = x + 1 - 2 * xp
    sib = c + 1 - 2 * k

    def remote(src, dst, send, recv, where):
        return pltpu.make_async_remote_copy(
            src_ref=src, dst_ref=dst, send_sem=send, recv_sem=recv, device_id=where, device_id_type=MESH
        )

    barrier = pltpu.get_barrier_semaphore()

    def greet_ctx(i, _):
        pl.semaphore_signal(barrier, inc=1, device_id={"ctx": lax.rem(c + i, NC)}, device_id_type=MESH)
        return 0

    lax.fori_loop(1, NC, greet_ctx, 0)
    for i in range(1, NT):
        pl.semaphore_signal(barrier, inc=1, device_id={"tp": lax.rem(t + i, NT)}, device_id_type=MESH)
    for i in range(NT):
        pl.semaphore_signal(barrier, inc=1, device_id={"dp": xq, "tp": lax.rem(t + i, NT)}, device_id_type=MESH)
    pl.semaphore_wait(barrier, NC - 1 + NT - 1 + NT)

    def kv_copy(i):
        if i == 0:
            g, slot, to = 1 - k, 4 + k, sib
        else:
            hop, g = (i + 1) // 2, (i + 1) % 2
            slot, to = 4 - 2 * hop + k, 2 * lax.rem(z + hop, NZ) + g
        return remote(
            kv_ref.at[:, pl.ds(mult(g * 256, 256), 256)], kvb.at[slot], kv_s.at[i], kv_r.at[slot], {"ctx": to}
        )

    def kv_arrival(slot):
        return remote(kvb.at[slot], kvb.at[slot], kv_s.at[0], kv_r.at[slot], {"ctx": sib})

    q_copy = remote(
        q_ref.at[:, pl.ds(mult((1 - k) * GW, GW), GW)], qbuf.at[k], q_s.at[0], q_r.at[0], {"ctx": sib}
    )
    q_arrival = remote(qbuf.at[1 - k], qbuf.at[1 - k], q_s.at[0], q_r.at[0], {"ctx": sib})

    def w_place(zz, j):
        return wbuf.at[zz // 2, pl.ds(j * 1024, 1024), pl.ds(mult(lax.rem(zz, 2) * 128, 128), 128)]

    def w_index(up, s, j):
        return ((0 if up else 3) + s - 1) * 2 + j

    def w_copy(up, s, j):
        zz = lax.rem(z + (NZ - s + 1 if up else s - 1), NZ)
        to = 2 * lax.rem(z + (1 if up else NZ - 1), NZ) + k
        n = w_index(up, s, j)
        src = w_ref.at[pl.ds(j * 1024, 1024), pl.ds(mult(xp * 128, 128), 128)] if s == 1 else w_place(zz, j)
        return remote(src, w_place(zz, j), w_s.at[n], w_r.at[n], {"ctx": to})

    def w_arrived(up, s, j):
        zz = lax.rem(z + (NZ - s if up else s), NZ)
        n = w_index(up, s, j)
        remote(w_place(zz, j), w_place(zz, j), w_s.at[n], w_r.at[n], {"ctx": sib}).wait_recv()
        if s < (3 if up else 4):
            w_copy(up, s + 1, j).start()

    local_copies = [
        pltpu.make_async_copy(q_ref.at[:, pl.ds(mult(k * GW, GW), GW)], qbuf.at[k], loc.at[0]),
        pltpu.make_async_copy(kv_ref.at[:, pl.ds(mult(k * 256, 256), 256)], kvb.at[4 + k], loc.at[1]),
        pltpu.make_async_copy(w_ref.at[:, pl.ds(mult(xp * 128, 128), 128)],
                              wbuf.at[z // 2, :, pl.ds(mult(lax.rem(z, 2) * 128, 128), 128)], loc.at[2]),
        pltpu.make_async_copy(meta_ref, mbuf.at[c], loc.at[3]),
    ]

    def m_copy(i):
        return remote(meta_ref, mbuf.at[c], m_s.at[i], m_r.at[i], {"ctx": lax.rem(c + i, NC)})

    for i in (1, 2, 3, 4, 0):
        kv_copy(i).start()
    q_copy.start()
    for copy in local_copies:
        copy.start()
    w_copy(False, 1, 0).start()
    w_copy(False, 1, 1).start()

    def m_send(i, _):
        m_copy(i).start()
        return 0

    lax.fori_loop(1, NC, m_send, 0)

    ends = []
    total = jnp.int32(0)
    for d in range(8):
        total = total + len_ref[d]
        ends.append(total)
    for s in range(2):
        base = z * 512 + s * 256
        rows = lax.broadcasted_iota(jnp.int32, (TOK, 1), 0)
        start = jnp.zeros((TOK, 1), jnp.int32)
        for e in ends:
            start = jnp.where(rows + base >= e, e, start)
        keys = lax.broadcasted_iota(jnp.int32, (TOK, NK), 1)
        seen = (keys <= rows + 1024) & (keys >= start - (base - 1024))
        bias[s] = jnp.where(seen, 0.0, -1e30).astype(F32)

    w_arrived(False, 1, 0)
    w_arrived(False, 1, 1)
    for i in (1, 2, 3, 4):
        kv_copy(i).wait_send()
    w_copy(True, 1, 0).start()
    w_copy(True, 1, 1).start()
    for copy in local_copies:
        copy.wait()
    q_arrival.wait_recv()
    kv_arrival(5 - k).wait_recv()
    for slot in range(4):
        kv_arrival(slot).wait_recv()
    vo[:, :, 0:HS] = kvb[:, :, HS:]
    vo[:, :, HS:] = jnp.ones((6, TOK, HS), BF)

    def h_lanes(j, kk):
        return pl.ds(mult(kk * GW + j * 256, 256), 256)

    def h_to_partner(j):
        return remote(hbuf.at[:, 0, :, h_lanes(j, k)], hbuf.at[:, 1, :, h_lanes(j, k)],
                      h_s.at[0, j], h_r.at[0, j], {"dp": xq})

    def h_to_sibling(j):
        return remote(hbuf.at[:, 0, :, h_lanes(j, k)], hbuf.at[:, 0, :, h_lanes(j, k)],
                      h_s.at[1, j], h_r.at[1, j], {"ctx": sib})

    def h_forward(j):
        return remote(hbuf.at[:, 1, :, h_lanes(j, k)], hbuf.at[:, 1, :, h_lanes(j, k)],
                      h_s.at[2, j], h_r.at[2, j], {"ctx": sib})

    def h_arrival(j, way):
        if way == 0:
            place = hbuf.at[:, 1, :, h_lanes(j, k)]
        else:
            place = hbuf.at[:, way - 1, :, h_lanes(j, 1 - k)]
        return remote(place, place, h_s.at[way, j], h_r.at[way, j], {"ctx": sib})

    def attend(j):
        def unit(i, _):
            s = i // 2
            h = 2 * j + lax.rem(i, 2)
            q = qbuf[s, :, pl.ds(mult(h * HS, HS), HS)]
            keys = kvb[pl.ds(s, 5), :, 0:HS].reshape(NK, HS)
            scores = lax.dot_general(q, keys, (((1,), (1,)), ((), ())), preferred_element_type=F32)
            scores = scores * SCALE + bias[s]
            peak = jnp.max(scores, axis=1, keepdims=True)
            weights = jnp.exp2(scores - peak).astype(BF)
            mixed = jnp.dot(weights, vo[pl.ds(s, 5)].reshape(NK, 2 * HS), preferred_element_type=F32)
            hbuf[s, 0, :, pl.ds(mult(k * GW + h * HS, HS), HS)] = (mixed[:, :HS] / mixed[:, HS:]).astype(BF)
            return 0

        lax.fori_loop(0, 4, unit, 0)
        h_to_partner(j).start()
        h_to_sibling(j).start()

    def h_pass_on(j):
        h_arrival(j, 0).wait_recv()
        h_forward(j).start()

    attend(0)
    w_arrived(False, 2, 0)
    attend(1)
    w_arrived(False, 2, 1)
    w_arrived(True, 1, 0)
    attend(2)
    attend(3)
    w_arrived(True, 1, 1)
    w_arrived(False, 3, 0)
    h_pass_on(0)
    h_pass_on(1)
    w_arrived(False, 3, 1)
    w_arrived(True, 2, 0)

    def m_wait(i, _):
        src = lax.rem(c + NC - i, NC)
        remote(mbuf.at[src], mbuf.at[src], m_s.at[i], m_r.at[i], {"ctx": sib}).wait_recv()
        return 0

    lax.fori_loop(1, NC, m_wait, 0)
    table = pltpu.make_async_copy(mbuf, msm, loc.at[4])
    table.start()
    table.wait()

    def choose(i, _):
        cc = lax.rem(c + i, NC)
        row = lax.broadcasted_iota(jnp.int32, (32, TOK), 0)
        column = lax.broadcasted_iota(jnp.int32, (32, TOK), 1)
        for s in range(2):
            one = msm[2 * z + s, 0, cc] * 16
            two = msm[2 * z + s, 0, NC + cc] * 16 - 16
            wanted = row + jnp.where(row < 16, one, two)
            sel[s, pl.ds(mult(i * 32, 32), 32), :] = jnp.where(column == wanted, 1.0, 0.0).astype(BF)
        return 0

    lax.fori_loop(0, NC, choose, 0)
    counts = []
    count = jnp.int32(0)
    for n in range(NC):
        count = count + msm[n, 0, 2 * NC + c]
        counts.append(count)

    def place(r, _):
        src = jnp.int32(0)
        for n in range(NC - 1):
            src = src + jnp.where(counts[n] <= r, 1, 0)
        row = lax.broadcasted_iota(jnp.int32, (32, 512), 0)
        column = lax.broadcasted_iota(jnp.int32, (32, 512), 1)
        take[pl.ds(mult(r * 32, 32), 32), :] = jnp.where(column == row + src * 32, 1.0, 0.0).astype(BF)
        return 0

    lax.fori_loop(0, 8, place, 0)

    w_arrived(True, 2, 1)
    w_arrived(False, 4, 0)
    h_pass_on(2)
    w_arrived(False, 4, 1)
    h_pass_on(3)
    w_arrived(True, 3, 0)
    w_arrived(True, 3, 1)
    for j in range(4):
        h_arrival(j, 1).wait_recv()
        h_arrival(j, 2).wait_recv()

    def y_partner(s, i):
        tt = lax.rem(t + 1 + i, NT)
        return remote(pbuf.at[s, tt, 1], rbuf.at[s, 3 + i], y_s.at[s, 3 + i], y_r.at[s, 3 + i], {"dp": xq, "tp": tt})

    def y_own(s, i):
        tt = lax.rem(t + 1 + i, NT)
        return remote(pbuf.at[s, tt, 0], rbuf.at[s, i], y_s.at[s, i], y_r.at[s, i], {"tp": tt})

    for s in range(2):
        def product(i, _):
            tt = lax.rem(t + 1 + i, NT)
            part = jnp.dot(hbuf[s].reshape(2 * TOK, 2 * GW), wbuf[tt], preferred_element_type=F32)
            pbuf[s, tt] = part.astype(BF).reshape(2, TOK, 256)
            y_partner(s, i).start()

            @pl.when(i < NT - 1)
            def _():
                y_own(s, i).start()

            return 0

        lax.fori_loop(0, NT, product, 0)

    def g_copy(s, i):
        return remote(sbuf.at[s, i], gbuf.at[k, 2 * z + s], g_s.at[s, i], g_r.at[s, i], {"ctx": lax.rem(c + i, NC)})

    for s in range(2):
        for i in range(7):
            remote(rbuf.at[s, i], rbuf.at[s, i], y_s.at[s, i], y_r.at[s, i], {"ctx": sib}).wait_recv()
        own = pbuf[s, t, 0].astype(F32)
        for i in range(3):
            own = own + rbuf[s, i].astype(F32)
        red[s, :, 0:256] = own.astype(BF)
        other = rbuf[s, 3].astype(F32)
        for i in range(4, 7):
            other = other + rbuf[s, i].astype(F32)
        red[s, :, 256:512] = other.astype(BF)

        sbuf[s] = jnp.dot(sel[s], red[s], preferred_element_type=F32).astype(BF).reshape(NC, 32, 512)

        def send(i, _):
            g_copy(s, i).start()
            return 0

        lax.fori_loop(1, NC, send, 0)
        gbuf[k, 2 * z + s] = sbuf[s, 0]

    def g_wait(i, _):
        src = lax.rem(c + NC - i, NC)
        for s in range(2):
            place = gbuf.at[lax.rem(src, 2), 2 * (src // 2) + s]
            remote(place, place, g_s.at[s, i], g_r.at[s, i], {"ctx": sib}).wait_recv()
        return 0

    lax.fori_loop(1, NC, g_wait, 0)

    for kk in range(2):
        rows = jnp.dot(take[...], gbuf[kk].reshape(2 * TOK, 512), preferred_element_type=F32).astype(BF)
        first, second = rows[:, :256], rows[:, 256:]
        low = jnp.where(xp == 0, first, second)
        high = jnp.where(xp == 0, second, first)
        for a in range(2):
            at = a * 512 + kk * 256
            out_ref[:, at : at + 128] = low[:, a * 128 : a * 128 + 128]
            out_ref[:, at + 128 : at + 256] = high[:, a * 128 : a * 128 + 128]

    kv_copy(0).wait_send()
    q_copy.wait_send()
    for s in range(1, 5):
        for j in range(2):
            w_copy(False, s, j).wait_send()
            if s < 4:
                w_copy(True, s, j).wait_send()
    for j in range(4):
        h_to_partner(j).wait_send()
        h_to_sibling(j).wait_send()
        h_forward(j).wait_send()
    for s in range(2):
        for i in range(NT):
            y_partner(s, i).wait_send()
            if i < NT - 1:
                y_own(s, i).wait_send()

    def sent(i, _):
        m_copy(i).wait_send()
        g_copy(0, i).wait_send()
        g_copy(1, i).wait_send()
        return 0

    lax.fori_loop(1, NC, sent, 0)


def local(queries, key_value_vectors, out_weight, doc_lengths, shard_of):
    owner = shard_of.reshape(NC, 16)[:, 0]
    block = jnp.arange(NC, dtype=jnp.int32)
    hit = owner[:, None] == block[None, :]
    first = jnp.min(jnp.where(hit, block[:, None], NC - 1), axis=0)
    second = jnp.max(jnp.where(hit, block[:, None], 0), axis=0)
    sends = jnp.max(hit.astype(jnp.int32), axis=0)
    row = jnp.concatenate([first, second, sends, jnp.zeros((128 - 3 * NC,), jnp.int32)])
    meta = jnp.broadcast_to(row[None, :], (8, 128))
    dma = pltpu.SemaphoreType.DMA
    return pl.pallas_call(
        kernel,
        out_shape=jax.ShapeDtypeStruct((TOK, 1024), BF),
        in_specs=[pl.BlockSpec(memory_space=pl.ANY)] * 4 + [pl.BlockSpec(memory_space=pltpu.SMEM)],
        out_specs=pl.BlockSpec(memory_space=pltpu.VMEM),
        scratch_shapes=[
            pltpu.VMEM((2, TOK, GW), BF),
            pltpu.VMEM((6, TOK, 256), BF),
            pltpu.VMEM((6, TOK, 256), BF),
            pltpu.VMEM((2, TOK, NK), F32),
            pltpu.VMEM((2, 2, TOK, 2 * GW), BF),
            pltpu.VMEM((NT, 2 * GW, 256), BF),
            pltpu.VMEM((2, NT, 2, TOK, 256), BF),
            pltpu.VMEM((2, 7, TOK, 256), BF),
            pltpu.VMEM((2, TOK, 512), BF),
            pltpu.VMEM((2, NC, 32, 512), BF),
            pltpu.VMEM((2, NC, 32, 512), BF),
            pltpu.VMEM((2, 512, TOK), BF),
            pltpu.VMEM((TOK, 512), BF),
            pltpu.VMEM((NC, 8, 128), jnp.int32),
            pltpu.SMEM((NC, 8, 128), jnp.int32),
            dma((5,)),
            dma((NC,)), dma((NC,)),
            dma((1,)), dma((1,)),
            dma((5,)), dma((6,)),
            dma((14,)), dma((14,)),
            dma((3, 4)), dma((3, 4)),
            dma((2, 7)), dma((2, 7)),
            dma((2, NC)), dma((2, NC)),
        ],
        compiler_params=pltpu.CompilerParams(
            collective_id=0, has_side_effects=True, vmem_limit_bytes=56 * 1024 * 1024
        ),
        cost_estimate=pl.CostEstimate(flops=7_000_000_000, bytes_accessed=4_000_000, transcendentals=5_000_000),
    )(queries, key_value_vectors, out_weight, meta, doc_lengths)


def solution(mesh):
    placed = (
        P(("dp", "ctx"), "tp"),
        P(("dp", "ctx"), "tp"),
        P("tp", "ctx"),
        P("dp"),
        P(("dp", "ctx")),
    )
    return jax.shard_map(
        local, mesh=mesh, in_specs=placed, out_specs=P(("dp", "ctx"), "tp"), check_vma=False
    )
```

time: 323 us -> 115 us (0.36)
  the two profiles are of different devices: /device:TPU:1 before, /device:TPU:21 now
where the time goes in v1:
time: 115 us
  Pallas kernels  111 us (97%)
  local copies, waits for them, and re-layouts  3.34 us (3%)
    pallas_call x1, Pallas kernels, local(): pl.pallas_call(kernel, out_shape=jax.ShapeDtypeStruct((TOK, 1024), BF), i...  111 us

profile of v1, /device:TPU:21, one launch (start us, length us, event | category | flops | bytes accessed | tf_op | source)
XLA Modules:
  0.0 114.7 jit_solution(12606735356983894538)
XLA Ops:
  0.0 0.8 reshape.4
  0.8 0.1 slice_reduce_fusion
  0.9 0.1 select_reduce_fusion.1
  1.0 0.1 pad_add_fusion
  1.1 0.6 broadcast_in_dim.37.meta_ref
  1.7 111.2 %shard_map.55 = bf16[256,1024]{1,0:T(8,128)(2,1)} custom-call(bf16[256,2048]{1,0:T(8,128)(2,1)} %q_ref.1, bf16[256,512]{1,0:T(8,128)(2,1)} %kv_ref.1, bf16[2048,256]{1,0:T(8,128)(2,1)} %w_ref.1, s32[8,128]{1,0:T(8,128)} %broadcast_in_dim.37.meta_ref, s32[8]{0:T(128)} %len_ref.1), custom_call_target="tpu_custom_call" | custom-call | flops 7000000000 | bytes 4000000 | tf_op jit(solution)/shard_map/pallas_call | solution.py:363
  112.8 1.9 %copy.7 = bf16[256,1024]{1,0:T(8,128)(2,1)} copy(bf16[256,1024]{1,0:T(8,128)(2,1)} %shard_map.55) | data formatting | bytes 1048576
  (1 shorter events, 0.0 us)

commit v2 on v1

--- a/solution.py
+++ b/solution.py
@@ -19,6 +19,9 @@
 NZ = 8
 NC = 16
 NT = 4
+UP, DOWN = 2, 5
+SHARED = 768
+BOTH = 2 * GW - 2 * SHARED
 
 
 def mult(value, of):
@@ -38,6 +41,9 @@
     xp = lax.rem(x, 2)
     xq = x + 1 - 2 * xp
     sib = c + 1 - 2 * k
+    xs = 3 - x
+    half = lax.rem(x + x // 2, 2)
+    upper = x // 2
 
     def remote(src, dst, send, recv, where):
         return pltpu.make_async_remote_copy(
@@ -55,7 +61,8 @@
         pl.semaphore_signal(barrier, inc=1, device_id={"tp": lax.rem(t + i, NT)}, device_id_type=MESH)
     for i in range(NT):
         pl.semaphore_signal(barrier, inc=1, device_id={"dp": xq, "tp": lax.rem(t + i, NT)}, device_id_type=MESH)
-    pl.semaphore_wait(barrier, NC - 1 + NT - 1 + NT)
+    pl.semaphore_signal(barrier, inc=1, device_id={"dp": xs}, device_id_type=MESH)
+    pl.semaphore_wait(barrier, NC - 1 + NT - 1 + NT + 1)
 
     def kv_copy(i):
         if i == 0:
@@ -75,30 +82,54 @@
     )
     q_arrival = remote(qbuf.at[1 - k], qbuf.at[1 - k], q_s.at[0], q_r.at[0], {"ctx": sib})
 
-    def w_place(zz, j):
-        return wbuf.at[zz // 2, pl.ds(j * 1024, 1024), pl.ds(mult(lax.rem(zz, 2) * 128, 128), 128)]
-
-    def w_index(up, s, j):
-        return ((0 if up else 3) + s - 1) * 2 + j
+    def w_rows(j, mine=True):
+        if j == 0:
+            return pl.ds(mult((upper if mine else 1 - upper) * SHARED, SHARED), SHARED)
+        return pl.ds(2 * SHARED, BOTH)
+
+    def w_place(zz, rows):
+        return wbuf.at[zz // 2, rows, pl.ds(mult(lax.rem(zz, 2) * 128, 128), 128)]
+
+    def w_block(up, s):
+        return lax.rem(z + (NZ - s if up else s), NZ)
+
+    def w_index(up, s):
+        return (0 if up else UP) + s - 1
 
     def w_copy(up, s, j):
-        zz = lax.rem(z + (NZ - s + 1 if up else s - 1), NZ)
+        zz = w_block(up, s - 1)
         to = 2 * lax.rem(z + (1 if up else NZ - 1), NZ) + k
-        n = w_index(up, s, j)
-        src = w_ref.at[pl.ds(j * 1024, 1024), pl.ds(mult(xp * 128, 128), 128)] if s == 1 else w_place(zz, j)
-        return remote(src, w_place(zz, j), w_s.at[n], w_r.at[n], {"ctx": to})
-
-    def w_arrived(up, s, j):
-        zz = lax.rem(z + (NZ - s if up else s), NZ)
-        n = w_index(up, s, j)
-        remote(w_place(zz, j), w_place(zz, j), w_s.at[n], w_r.at[n], {"ctx": sib}).wait_recv()
-        if s < (3 if up else 4):
-            w_copy(up, s + 1, j).start()
+        n = w_index(up, s)
+        place = w_place(zz, w_rows(j))
+        src = w_ref.at[w_rows(j), pl.ds(mult(half * 128, 128), 128)] if s == 1 else place
+        return remote(src, place, w_s.at[n, j], w_r.at[n, j], {"ctx": to})
+
+    def w_share(up, s):
+        n = w_index(up, s)
+        place = w_place(w_block(up, s), w_rows(0))
+        return remote(place, place, w_s.at[n, 2], w_r.at[n, 2], {"dp": xs})
+
+    def w_shared(up, s):
+        n = w_index(up, s)
+        place = w_place(w_block(up, s), w_rows(0, False))
+        return remote(place, place, w_s.at[n, 2], w_r.at[n, 2], {"dp": xs})
+
+    def w_arrived(up, s):
+        n = w_index(up, s)
+        for j in range(2):
+            place = w_place(w_block(up, s), w_rows(j))
+            remote(place, place, w_s.at[n, j], w_r.at[n, j], {"ctx": sib}).wait_recv()
+            if s < (UP if up else DOWN):
+                w_copy(up, s + 1, j).start()
+            if j == 0:
+                w_share(up, s).start()
+
+    w_steps = [(True, s) for s in range(1, UP + 1)] + [(False, s) for s in range(1, DOWN + 1)]
 
     local_copies = [
         pltpu.make_async_copy(q_ref.at[:, pl.ds(mult(k * GW, GW), GW)], qbuf.at[k], loc.at[0]),
         pltpu.make_async_copy(kv_ref.at[:, pl.ds(mult(k * 256, 256), 256)], kvb.at[4 + k], loc.at[1]),
-        pltpu.make_async_copy(w_ref.at[:, pl.ds(mult(xp * 128, 128), 128)],
+        pltpu.make_async_copy(w_ref.at[:, pl.ds(mult(half * 128, 128), 128)],
                               wbuf.at[z // 2, :, pl.ds(mult(lax.rem(z, 2) * 128, 128), 128)], loc.at[2]),
         pltpu.make_async_copy(meta_ref, mbuf.at[c], loc.at[3]),
     ]
@@ -106,13 +137,19 @@
     def m_copy(i):
         return remote(meta_ref, mbuf.at[c], m_s.at[i], m_r.at[i], {"ctx": lax.rem(c + i, NC)})
 
-    for i in (1, 2, 3, 4, 0):
+    for i in (1, 2, 0):
         kv_copy(i).start()
+
+    @pl.when(k == 1)
+    def _():
+        kv_copy(3).start()
+        kv_copy(4).start()
+
+    w_copy(False, 1, 0).start()
+    w_copy(False, 1, 1).start()
     q_copy.start()
     for copy in local_copies:
         copy.start()
-    w_copy(False, 1, 0).start()
-    w_copy(False, 1, 1).start()
 
     def m_send(i, _):
         m_copy(i).start()
@@ -135,78 +172,90 @@
         seen = (keys <= rows + 1024) & (keys >= start - (base - 1024))
         bias[s] = jnp.where(seen, 0.0, -1e30).astype(F32)
 
-    w_arrived(False, 1, 0)
-    w_arrived(False, 1, 1)
+    kv_arrival(2).wait_recv()
+    kv_arrival(3).wait_recv()
+
+    @pl.when(k == 0)
+    def _():
+        kv_copy(3).start()
+        kv_copy(4).start()
+
+    for copy in local_copies:
+        copy.wait()
+    q_arrival.wait_recv()
+    kv_arrival(5 - k).wait_recv()
+    w_arrived(False, 1)
+
+    def widen(slot, count):
+        vo[slot : slot + count, :, 0:HS] = kvb[slot : slot + count, :, HS:]
+        vo[slot : slot + count, :, HS:] = jnp.ones((count, TOK, HS), BF)
+
+    widen(2, 4)
+    kv_arrival(1).wait_recv()
+    widen(1, 1)
+
+    def h_lanes(j, kk):
+        return pl.ds(mult(kk * GW + j * 256, 256), 256)
+
+    def h_to_partner(s, j):
+        return remote(hbuf.at[s, 0, :, h_lanes(j, k)], hbuf.at[s, 1, :, h_lanes(j, k)],
+                      h_s.at[0, s, j], h_r.at[0, s, j], {"dp": xq})
+
+    def h_to_sibling(s, j):
+        place = hbuf.at[s, 0, :, h_lanes(j, k)]
+        return remote(place, place, h_s.at[1, s, j], h_r.at[1, s, j], {"ctx": sib})
+
+    def h_forward(s, j):
+        place = hbuf.at[s, 1, :, h_lanes(j, k)]
+        return remote(place, place, h_s.at[2, s, j], h_r.at[2, s, j], {"ctx": sib})
+
+    def h_arrival(s, j, way):
+        place = hbuf.at[s, 1, :, h_lanes(j, k)] if way == 0 else hbuf.at[s, way - 1, :, h_lanes(j, 1 - k)]
+        return remote(place, place, h_s.at[way, s, j], h_r.at[way, s, j], {"ctx": sib})
+
+    def attend(s, j):
+        keys = kvb[s : s + 5, :, 0:HS].reshape(NK, HS)
+        values = vo[s : s + 5].reshape(NK, 2 * HS)
+        heads = (2 * j, 2 * j + 1)
+        scores = [
+            lax.dot_general(qbuf[s, :, h * HS : (h + 1) * HS], keys, (((1,), (1,)), ((), ())),
+                            preferred_element_type=F32)
+            for h in heads
+        ]
+        for h, score in zip(heads, scores):
+            score = score * SCALE + bias[s]
+            weights = jnp.exp2(score - jnp.max(score, axis=1, keepdims=True)).astype(BF)
+            mixed = jnp.dot(weights, values, preferred_element_type=F32)
+            hbuf[s, 0, :, pl.ds(mult(k * GW + h * HS, HS), HS)] = (mixed[:, :HS] / mixed[:, HS:]).astype(BF)
+        h_to_partner(s, j).start()
+        h_to_sibling(s, j).start()
+
+    def h_pass_on(s, j):
+        h_arrival(s, j, 0).wait_recv()
+        h_forward(s, j).start()
+
+    attend(1, 0)
+    w_arrived(False, 2)
+    attend(1, 1)
+    attend(1, 2)
+    attend(1, 3)
     for i in (1, 2, 3, 4):
         kv_copy(i).wait_send()
     w_copy(True, 1, 0).start()
     w_copy(True, 1, 1).start()
-    for copy in local_copies:
-        copy.wait()
-    q_arrival.wait_recv()
-    kv_arrival(5 - k).wait_recv()
-    for slot in range(4):
-        kv_arrival(slot).wait_recv()
-    vo[:, :, 0:HS] = kvb[:, :, HS:]
-    vo[:, :, HS:] = jnp.ones((6, TOK, HS), BF)
-
-    def h_lanes(j, kk):
-        return pl.ds(mult(kk * GW + j * 256, 256), 256)
-
-    def h_to_partner(j):
-        return remote(hbuf.at[:, 0, :, h_lanes(j, k)], hbuf.at[:, 1, :, h_lanes(j, k)],
-                      h_s.at[0, j], h_r.at[0, j], {"dp": xq})
-
-    def h_to_sibling(j):
-        return remote(hbuf.at[:, 0, :, h_lanes(j, k)], hbuf.at[:, 0, :, h_lanes(j, k)],
-                      h_s.at[1, j], h_r.at[1, j], {"ctx": sib})
-
-    def h_forward(j):
-        return remote(hbuf.at[:, 1, :, h_lanes(j, k)], hbuf.at[:, 1, :, h_lanes(j, k)],
-                      h_s.at[2, j], h_r.at[2, j], {"ctx": sib})
-
-    def h_arrival(j, way):
-        if way == 0:
-            place = hbuf.at[:, 1, :, h_lanes(j, k)]
-        else:
-            place = hbuf.at[:, way - 1, :, h_lanes(j, 1 - k)]
-        return remote(place, place, h_s.at[way, j], h_r.at[way, j], {"ctx": sib})
-
-    def attend(j):
-        def unit(i, _):
-            s = i // 2
-            h = 2 * j + lax.rem(i, 2)
-            q = qbuf[s, :, pl.ds(mult(h * HS, HS), HS)]
-            keys = kvb[pl.ds(s, 5), :, 0:HS].reshape(NK, HS)
-            scores = lax.dot_general(q, keys, (((1,), (1,)), ((), ())), preferred_element_type=F32)
-            scores = scores * SCALE + bias[s]
-            peak = jnp.max(scores, axis=1, keepdims=True)
-            weights = jnp.exp2(scores - peak).astype(BF)
-            mixed = jnp.dot(weights, vo[pl.ds(s, 5)].reshape(NK, 2 * HS), preferred_element_type=F32)
-            hbuf[s, 0, :, pl.ds(mult(k * GW + h * HS, HS), HS)] = (mixed[:, :HS] / mixed[:, HS:]).astype(BF)
-            return 0
-
-        lax.fori_loop(0, 4, unit, 0)
-        h_to_partner(j).start()
-        h_to_sibling(j).start()
-
-    def h_pass_on(j):
-        h_arrival(j, 0).wait_recv()
-        h_forward(j).start()
-
-    attend(0)
-    w_arrived(False, 2, 0)
-    attend(1)
-    w_arrived(False, 2, 1)
-    w_arrived(True, 1, 0)
-    attend(2)
-    attend(3)
-    w_arrived(True, 1, 1)
-    w_arrived(False, 3, 0)
-    h_pass_on(0)
-    h_pass_on(1)
-    w_arrived(False, 3, 1)
-    w_arrived(True, 2, 0)
+    kv_arrival(0).wait_recv()
+    widen(0, 1)
+    attend(0, 0)
+    h_pass_on(1, 0)
+    w_arrived(False, 3)
+    attend(0, 1)
+    h_pass_on(1, 1)
+    attend(0, 2)
+    h_pass_on(1, 2)
+    w_arrived(True, 1)
+    attend(0, 3)
+    h_pass_on(1, 3)
+    w_arrived(False, 4)
 
     def m_wait(i, _):
         src = lax.rem(c + NC - i, NC)
@@ -218,22 +267,31 @@
     table.start()
     table.wait()
 
-    def choose(i, _):
-        cc = lax.rem(c + i, NC)
-        row = lax.broadcasted_iota(jnp.int32, (32, TOK), 0)
-        column = lax.broadcasted_iota(jnp.int32, (32, TOK), 1)
-        for s in range(2):
-            one = msm[2 * z + s, 0, cc] * 16
-            two = msm[2 * z + s, 0, NC + cc] * 16 - 16
-            wanted = row + jnp.where(row < 16, one, two)
-            sel[s, pl.ds(mult(i * 32, 32), 32), :] = jnp.where(column == wanted, 1.0, 0.0).astype(BF)
-        return 0
-
-    lax.fori_loop(0, NC, choose, 0)
+    def owner(n, b):
+        return msm[n, b // 8, (b % 8) * 16]
+
+    lane = lax.broadcasted_iota(jnp.int32, (1, TOK), 1)
+    for s in range(2):
+        owners = [owner(2 * z + s, b) for b in range(16)]
+        wanted = jnp.zeros((1, TOK), jnp.int32)
+        for b in range(16):
+            second = jnp.int32(0)
+            for e in range(b):
+                second = second + jnp.where(owners[e] == owners[b], 16, 0)
+            slot = owners[b] - c
+            slot = jnp.where(slot < 0, slot + NC, slot)
+            wanted = jnp.where(lane // 16 == b, slot * 32 + second, wanted)
+        wanted = wanted + lax.rem(lane, 16)
+        row = lax.broadcasted_iota(jnp.int32, (512, TOK), 0)
+        sel[s] = jnp.where(row == wanted, 1.0, 0.0).astype(BF)
+
     counts = []
     count = jnp.int32(0)
     for n in range(NC):
-        count = count + msm[n, 0, 2 * NC + c]
+        any_block = jnp.int32(0)
+        for b in range(16):
+            any_block = jnp.maximum(any_block, jnp.where(owner(n, b) == c, 1, 0))
+        count = count + any_block
         counts.append(count)
 
     def place(r, _):
@@ -247,16 +305,18 @@
 
     lax.fori_loop(0, 8, place, 0)
 
-    w_arrived(True, 2, 1)
-    w_arrived(False, 4, 0)
-    h_pass_on(2)
-    w_arrived(False, 4, 1)
-    h_pass_on(3)
-    w_arrived(True, 3, 0)
-    w_arrived(True, 3, 1)
-    for j in range(4):
-        h_arrival(j, 1).wait_recv()
-        h_arrival(j, 2).wait_recv()
+    h_pass_on(0, 0)
+    h_pass_on(0, 1)
+    w_arrived(True, 2)
+    h_pass_on(0, 2)
+    w_arrived(False, 5)
+    h_pass_on(0, 3)
+    for up, s in w_steps:
+        w_shared(up, s).wait_recv()
+    for s in range(2):
+        for j in range(4):
+            h_arrival(s, j, 1).wait_recv()
+            h_arrival(s, j, 2).wait_recv()
 
     def y_partner(s, i):
         tt = lax.rem(t + 1 + i, NT)
@@ -317,8 +377,8 @@
     for kk in range(2):
         rows = jnp.dot(take[...], gbuf[kk].reshape(2 * TOK, 512), preferred_element_type=F32).astype(BF)
         first, second = rows[:, :256], rows[:, 256:]
-        low = jnp.where(xp == 0, first, second)
-        high = jnp.where(xp == 0, second, first)
+        low = jnp.where(half == 0, first, second)
+        high = jnp.where(half == 0, second, first)
         for a in range(2):
             at = a * 512 + kk * 256
             out_ref[:, at : at + 128] = low[:, a * 128 : a * 128 + 128]
@@ -326,15 +386,15 @@
 
     kv_copy(0).wait_send()
     q_copy.wait_send()
-    for s in range(1, 5):
-        for j in range(2):
-            w_copy(False, s, j).wait_send()
-            if s < 4:
-                w_copy(True, s, j).wait_send()
-    for j in range(4):
-        h_to_partner(j).wait_send()
-        h_to_sibling(j).wait_send()
-        h_forward(j).wait_send()
+    for up, s in w_steps:
+        w_copy(up, s, 0).wait_send()
+        w_copy(up, s, 1).wait_send()
+        w_share(up, s).wait_send()
+    for s in range(2):
+        for j in range(4):
+            h_to_partner(s, j).wait_send()
+            h_to_sibling(s, j).wait_send()
+            h_forward(s, j).wait_send()
     for s in range(2):
         for i in range(NT):
             y_partner(s, i).wait_send()
@@ -351,14 +411,7 @@
 
 
 def local(queries, key_value_vectors, out_weight, doc_lengths, shard_of):
-    owner = shard_of.reshape(NC, 16)[:, 0]
-    block = jnp.arange(NC, dtype=jnp.int32)
-    hit = owner[:, None] == block[None, :]
-    first = jnp.min(jnp.where(hit, block[:, None], NC - 1), axis=0)
-    second = jnp.max(jnp.where(hit, block[:, None], 0), axis=0)
-    sends = jnp.max(hit.astype(jnp.int32), axis=0)
-    row = jnp.concatenate([first, second, sends, jnp.zeros((128 - 3 * NC,), jnp.int32)])
-    meta = jnp.broadcast_to(row[None, :], (8, 128))
+    meta = shard_of.reshape(2, 128)
     dma = pltpu.SemaphoreType.DMA
     return pl.pallas_call(
         kernel,
@@ -379,14 +432,14 @@
             pltpu.VMEM((2, NC, 32, 512), BF),
             pltpu.VMEM((2, 512, TOK), BF),
             pltpu.VMEM((TOK, 512), BF),
-            pltpu.VMEM((NC, 8, 128), jnp.int32),
-            pltpu.SMEM((NC, 8, 128), jnp.int32),
+            pltpu.VMEM((NC, 2, 128), jnp.int32),
+            pltpu.SMEM((NC, 2, 128), jnp.int32),
             dma((5,)),
             dma((NC,)), dma((NC,)),
             dma((1,)), dma((1,)),
             dma((5,)), dma((6,)),
-            dma((14,)), dma((14,)),
-            dma((3, 4)), dma((3, 4)),
+            dma((7, 3)), dma((7, 3)),
+            dma((3, 2, 4)), dma((3, 2, 4)),
             dma((2, 7)), dma((2, 7)),
             dma((2, NC)), dma((2, NC)),
         ],

time: 115 us -> 105 us (0.913)
  the two profiles are of different devices: /device:TPU:21 before, /device:TPU:1 now
where the time goes in v2:
time: 105 us
  Pallas kernels  103 us (98%)
  local copies, waits for them, and re-layouts  1.87 us (2%)
    pallas_call x1, Pallas kernels, local(): pl.pallas_call(kernel, out_shape=jax.ShapeDtypeStruct((TOK, 1024), BF), i...  103 us

profile of v2, /device:TPU:1, one launch (start us, length us, event | category | flops | bytes accessed | tf_op | source)
XLA Modules:
  0.0 105.0 jit_solution(15323453330586197984)
XLA Ops:
  0.0 103.1 %shard_map.55 = bf16[256,1024]{1,0:T(8,128)(2,1)} custom-call(bf16[256,2048]{1,0:T(8,128)(2,1)} %q_ref.1, bf16[256,512]{1,0:T(8,128)(2,1)} %kv_ref.1, bf16[2048,256]{1,0:T(8,128)(2,1)} %w_ref.1, s32[2,128]{1,0:T(2,128)} %bitcast.1, s32[8]{0:T(128)} %len_ref.1), custom_call_target="tpu_custom_call" | custom-call | flops 7000000000 | bytes 4000000 | tf_op jit(solution)/shard_map/pallas_call | solution.py:416
  103.1 1.9 %copy.7 = bf16[256,1024]{1,0:T(8,128)(2,1)} copy(bf16[256,1024]{1,0:T(8,128)(2,1)} %shard_map.55) | data formatting | bytes 1048576

commit v3 on v2

--- a/solution.py
+++ b/solution.py
@@ -19,8 +19,8 @@
 NZ = 8
 NC = 16
 NT = 4
-UP, DOWN = 2, 5
-SHARED = 768
+UP, DOWN = 3, 5
+SHARED = 704
 BOTH = 2 * GW - 2 * SHARED
 
 
@@ -30,7 +30,7 @@
 
 def kernel(
     q_ref, kv_ref, w_ref, meta_ref, len_ref, out_ref,
-    qbuf, kvb, vo, bias, hbuf, wbuf, pbuf, rbuf, red, sbuf, gbuf, sel, take, mbuf, msm,
+    qbuf, kvb, vo, bias, hbuf, wbuf, pbuf, rbuf, sbuf, gbuf, sel, take, mbuf, msm,
     loc, m_s, m_r, q_s, q_r, kv_s, kv_r, w_s, w_r, h_s, h_r, y_s, y_r, g_s, g_r,
 ):
     x = lax.axis_index("dp")
@@ -84,7 +84,7 @@
 
     def w_rows(j, mine=True):
         if j == 0:
-            return pl.ds(mult((upper if mine else 1 - upper) * SHARED, SHARED), SHARED)
+            return pl.ds(mult((upper if mine else 1 - upper) * SHARED, 16), SHARED)
         return pl.ds(2 * SHARED, BOTH)
 
     def w_place(zz, rows):
@@ -114,15 +114,20 @@
         place = w_place(w_block(up, s), w_rows(0, False))
         return remote(place, place, w_s.at[n, 2], w_r.at[n, 2], {"dp": xs})
 
-    def w_arrived(up, s):
+    def w_parts(up, s):
+        return (1,) if up and s == UP else (0,) if not up and s == DOWN else (0, 1)
+
+    def w_start(up, s, j):
+        if s <= (UP if up else DOWN) and j in w_parts(up, s):
+            w_copy(up, s, j).start()
+
+    def w_arrived(up, s, j):
         n = w_index(up, s)
-        for j in range(2):
-            place = w_place(w_block(up, s), w_rows(j))
-            remote(place, place, w_s.at[n, j], w_r.at[n, j], {"ctx": sib}).wait_recv()
-            if s < (UP if up else DOWN):
-                w_copy(up, s + 1, j).start()
-            if j == 0:
-                w_share(up, s).start()
+        place = w_place(w_block(up, s), w_rows(j))
+        remote(place, place, w_s.at[n, j], w_r.at[n, j], {"ctx": sib}).wait_recv()
+        w_start(up, s + 1, j)
+        if j == 0:
+            w_share(up, s).start()
 
     w_steps = [(True, s) for s in range(1, UP + 1)] + [(False, s) for s in range(1, DOWN + 1)]
 
@@ -137,16 +142,25 @@
     def m_copy(i):
         return remote(meta_ref, mbuf.at[c], m_s.at[i], m_r.at[i], {"ctx": lax.rem(c + i, NC)})
 
-    for i in (1, 2, 0):
-        kv_copy(i).start()
+    kv_copy(0).start()
+    w_copy(False, 1, 0).start()
+    kv_copy(1).start()
+    kv_copy(2).start()
 
     @pl.when(k == 1)
     def _():
         kv_copy(3).start()
         kv_copy(4).start()
-
-    w_copy(False, 1, 0).start()
+        w_copy(True, 1, 0).start()
+
+    @pl.when(k == 0)
+    def _():
+        w_copy(True, 1, 0).start()
+        kv_copy(3).start()
+        kv_copy(4).start()
+
     w_copy(False, 1, 1).start()
+    w_copy(True, 1, 1).start()
     q_copy.start()
     for copy in local_copies:
         copy.start()
@@ -175,22 +189,18 @@
     kv_arrival(2).wait_recv()
     kv_arrival(3).wait_recv()
 
-    @pl.when(k == 0)
-    def _():
-        kv_copy(3).start()
-        kv_copy(4).start()
-
     for copy in local_copies:
         copy.wait()
     q_arrival.wait_recv()
     kv_arrival(5 - k).wait_recv()
-    w_arrived(False, 1)
-
     def widen(slot, count):
         vo[slot : slot + count, :, 0:HS] = kvb[slot : slot + count, :, HS:]
         vo[slot : slot + count, :, HS:] = jnp.ones((count, TOK, HS), BF)
 
     widen(2, 4)
+    w_arrived(False, 1, 0)
+    w_arrived(False, 1, 1)
+    w_arrived(False, 2, 0)
     kv_arrival(1).wait_recv()
     widen(1, 1)
 
@@ -235,27 +245,26 @@
         h_forward(s, j).start()
 
     attend(1, 0)
-    w_arrived(False, 2)
+    w_arrived(False, 2, 1)
     attend(1, 1)
+    w_arrived(True, 1, 0)
     attend(1, 2)
     attend(1, 3)
-    for i in (1, 2, 3, 4):
-        kv_copy(i).wait_send()
-    w_copy(True, 1, 0).start()
-    w_copy(True, 1, 1).start()
+    w_arrived(False, 3, 0)
     kv_arrival(0).wait_recv()
     widen(0, 1)
     attend(0, 0)
     h_pass_on(1, 0)
-    w_arrived(False, 3)
+    w_arrived(True, 1, 1)
+    w_arrived(False, 3, 1)
     attend(0, 1)
     h_pass_on(1, 1)
     attend(0, 2)
     h_pass_on(1, 2)
-    w_arrived(True, 1)
+    w_arrived(True, 2, 0)
+    w_arrived(False, 4, 0)
     attend(0, 3)
     h_pass_on(1, 3)
-    w_arrived(False, 4)
 
     def m_wait(i, _):
         src = lax.rem(c + NC - i, NC)
@@ -305,106 +314,109 @@
 
     lax.fori_loop(0, 8, place, 0)
 
+    w_arrived(False, 4, 1)
+    w_arrived(True, 2, 1)
     h_pass_on(0, 0)
     h_pass_on(0, 1)
-    w_arrived(True, 2)
+    w_arrived(False, 5, 0)
+    w_arrived(True, 3, 1)
     h_pass_on(0, 2)
-    w_arrived(False, 5)
     h_pass_on(0, 3)
     for up, s in w_steps:
-        w_shared(up, s).wait_recv()
+        if 0 in w_parts(up, s):
+            w_shared(up, s).wait_recv()
     for s in range(2):
         for j in range(4):
             h_arrival(s, j, 1).wait_recv()
             h_arrival(s, j, 2).wait_recv()
 
-    def y_partner(s, i):
-        tt = lax.rem(t + 1 + i, NT)
-        return remote(pbuf.at[s, tt, 1], rbuf.at[s, 3 + i], y_s.at[s, 3 + i], y_r.at[s, 3 + i], {"dp": xq, "tp": tt})
-
-    def y_own(s, i):
-        tt = lax.rem(t + 1 + i, NT)
-        return remote(pbuf.at[s, tt, 0], rbuf.at[s, i], y_s.at[s, i], y_r.at[s, i], {"tp": tt})
-
-    for s in range(2):
-        def product(i, _):
+    def y_copy(s, a, i):
+        own = i < NT - 1
+        tt = lax.rem(t + 1 + (i if own else i - NT + 1), NT)
+        where = {"tp": tt} if own else {"dp": xq, "tp": tt}
+        return remote(pbuf.at[s, tt, a, 0 if own else 1], rbuf.at[s, a, i], y_s.at[s, a, i], y_r.at[s, a, i], where)
+
+    for s in range(2):
+        for i in range(NT):
             tt = lax.rem(t + 1 + i, NT)
-            part = jnp.dot(hbuf[s].reshape(2 * TOK, 2 * GW), wbuf[tt], preferred_element_type=F32)
-            pbuf[s, tt] = part.astype(BF).reshape(2, TOK, 256)
-            y_partner(s, i).start()
-
-            @pl.when(i < NT - 1)
-            def _():
-                y_own(s, i).start()
-
-            return 0
-
-        lax.fori_loop(0, NT, product, 0)
-
-    def g_copy(s, i):
-        return remote(sbuf.at[s, i], gbuf.at[k, 2 * z + s], g_s.at[s, i], g_r.at[s, i], {"ctx": lax.rem(c + i, NC)})
-
-    for s in range(2):
-        for i in range(7):
-            remote(rbuf.at[s, i], rbuf.at[s, i], y_s.at[s, i], y_r.at[s, i], {"ctx": sib}).wait_recv()
-        own = pbuf[s, t, 0].astype(F32)
-        for i in range(3):
-            own = own + rbuf[s, i].astype(F32)
-        red[s, :, 0:256] = own.astype(BF)
-        other = rbuf[s, 3].astype(F32)
-        for i in range(4, 7):
-            other = other + rbuf[s, i].astype(F32)
-        red[s, :, 256:512] = other.astype(BF)
-
-        sbuf[s] = jnp.dot(sel[s], red[s], preferred_element_type=F32).astype(BF).reshape(NC, 32, 512)
-
-        def send(i, _):
-            g_copy(s, i).start()
-            return 0
-
-        lax.fori_loop(1, NC, send, 0)
-        gbuf[k, 2 * z + s] = sbuf[s, 0]
+            part = jnp.dot(hbuf[s].reshape(2 * TOK, 2 * GW), wbuf[tt], preferred_element_type=F32).astype(BF)
+            for a in range(2):
+                pbuf[s, tt, a] = part[:, a * 128 : a * 128 + 128].reshape(2, TOK, 128)
+            y_copy(s, 0, NT - 1 + i).start()
+            if i < NT - 1:
+                y_copy(s, 0, i).start()
+        for i in range(NT):
+            y_copy(s, 1, NT - 1 + i).start()
+            if i < NT - 1:
+                y_copy(s, 1, i).start()
+
+    def g_copy(s, e, i):
+        return remote(sbuf.at[s, e, i], gbuf.at[k, e, 2 * z + s], g_s.at[s, e, i], g_r.at[s, e, i],
+                      {"ctx": lax.rem(c + i, NC)})
+
+    for s in range(2):
+        for e in range(2):
+            for i in range(7):
+                place = rbuf.at[s, e, i]
+                remote(place, place, y_s.at[s, e, i], y_r.at[s, e, i], {"ctx": sib}).wait_recv()
+            own = pbuf[s, t, e, 0].astype(F32)
+            for i in range(3):
+                own = own + rbuf[s, e, i].astype(F32)
+            other = rbuf[s, e, 3].astype(F32)
+            for i in range(4, 7):
+                other = other + rbuf[s, e, i].astype(F32)
+            both = jnp.concatenate([own.astype(BF), other.astype(BF)], axis=1)
+            rows = jnp.dot(sel[s], both, preferred_element_type=F32)
+            sbuf[s, e] = rows.astype(BF).reshape(NC, 32, 256)
+
+            def send(i, _):
+                g_copy(s, e, i).start()
+                return 0
+
+            lax.fori_loop(1, NC, send, 0)
+            gbuf[k, e, 2 * z + s] = sbuf[s, e, 0]
 
     def g_wait(i, _):
         src = lax.rem(c + NC - i, NC)
         for s in range(2):
-            place = gbuf.at[lax.rem(src, 2), 2 * (src // 2) + s]
-            remote(place, place, g_s.at[s, i], g_r.at[s, i], {"ctx": sib}).wait_recv()
+            for e in range(2):
+                place = gbuf.at[lax.rem(src, 2), e, 2 * (src // 2) + s]
+                remote(place, place, g_s.at[s, e, i], g_r.at[s, e, i], {"ctx": sib}).wait_recv()
         return 0
 
     lax.fori_loop(1, NC, g_wait, 0)
 
     for kk in range(2):
-        rows = jnp.dot(take[...], gbuf[kk].reshape(2 * TOK, 512), preferred_element_type=F32).astype(BF)
-        first, second = rows[:, :256], rows[:, 256:]
-        low = jnp.where(half == 0, first, second)
-        high = jnp.where(half == 0, second, first)
         for a in range(2):
+            rows = jnp.dot(take[...], gbuf[kk, a].reshape(2 * TOK, 256), preferred_element_type=F32).astype(BF)
+            first, second = rows[:, :128], rows[:, 128:]
             at = a * 512 + kk * 256
-            out_ref[:, at : at + 128] = low[:, a * 128 : a * 128 + 128]
-            out_ref[:, at + 128 : at + 256] = high[:, a * 128 : a * 128 + 128]
-
-    kv_copy(0).wait_send()
+            out_ref[:, at : at + 128] = jnp.where(half == 0, first, second)
+            out_ref[:, at + 128 : at + 256] = jnp.where(half == 0, second, first)
+
+    for i in range(5):
+        kv_copy(i).wait_send()
     q_copy.wait_send()
     for up, s in w_steps:
-        w_copy(up, s, 0).wait_send()
-        w_copy(up, s, 1).wait_send()
-        w_share(up, s).wait_send()
+        for j in w_parts(up, s):
+            w_copy(up, s, j).wait_send()
+            if j == 0:
+                w_share(up, s).wait_send()
     for s in range(2):
         for j in range(4):
             h_to_partner(s, j).wait_send()
             h_to_sibling(s, j).wait_send()
             h_forward(s, j).wait_send()
     for s in range(2):
-        for i in range(NT):
-            y_partner(s, i).wait_send()
-            if i < NT - 1:
-                y_own(s, i).wait_send()
+        for a in range(2):
+            for i in range(7):
+                y_copy(s, a, i).wait_send()
 
     def sent(i, _):
         m_copy(i).wait_send()
-        g_copy(0, i).wait_send()
-        g_copy(1, i).wait_send()
+        for s in range(2):
+            for e in range(2):
+                g_copy(s, e, i).wait_send()
         return 0
 
     lax.fori_loop(1, NC, sent, 0)
@@ -425,11 +437,10 @@
             pltpu.VMEM((2, TOK, NK), F32),
             pltpu.VMEM((2, 2, TOK, 2 * GW), BF),
             pltpu.VMEM((NT, 2 * GW, 256), BF),
-            pltpu.VMEM((2, NT, 2, TOK, 256), BF),
-            pltpu.VMEM((2, 7, TOK, 256), BF),
-            pltpu.VMEM((2, TOK, 512), BF),
-            pltpu.VMEM((2, NC, 32, 512), BF),
-            pltpu.VMEM((2, NC, 32, 512), BF),
+            pltpu.VMEM((2, NT, 2, 2, TOK, 128), BF),
+            pltpu.VMEM((2, 2, 7, TOK, 128), BF),
+            pltpu.VMEM((2, 2, NC, 32, 256), BF),
+            pltpu.VMEM((2, 2, NC, 32, 256), BF),
             pltpu.VMEM((2, 512, TOK), BF),
             pltpu.VMEM((TOK, 512), BF),
             pltpu.VMEM((NC, 2, 128), jnp.int32),
@@ -438,10 +449,10 @@
             dma((NC,)), dma((NC,)),
             dma((1,)), dma((1,)),
             dma((5,)), dma((6,)),
-            dma((7, 3)), dma((7, 3)),
+            dma((8, 3)), dma((8, 3)),
             dma((3, 2, 4)), dma((3, 2, 4)),
-            dma((2, 7)), dma((2, 7)),
-            dma((2, NC)), dma((2, NC)),
+            dma((2, 2, 7)), dma((2, 2, 7)),
+            dma((2, 2, NC)), dma((2, 2, NC)),
         ],
         compiler_params=pltpu.CompilerParams(
             collective_id=0, has_side_effects=True, vmem_limit_bytes=56 * 1024 * 1024

time: 105 us -> 98.2 us (0.935); the launches traced: 105 us -> 97 us
  Pallas kernels: 103 us -> 95.2 us
    pallas_call x1, Pallas kernels: 103 us -> 95.2 us  [local(): pl.pallas_call(kernel, out_shape=jax.ShapeDtypeStruct((TOK, 1024), BF), i...]
where the time goes in v3:
time: 98.2 us; the launch traced here: 97 us
  Pallas kernels  95.2 us (97%)
  local copies, waits for them, and re-layouts  1.87 us (2%)
    pallas_call x1, Pallas kernels, local(): pl.pallas_call(kernel, out_shape=jax.ShapeDtypeStruct((TOK, 1024), BF), i...  95.2 us

profile of v3, /device:TPU:1, one launch (start us, length us, event | category | flops | bytes accessed | tf_op | source)
XLA Modules:
  0.0 97.0 jit_solution(14553905225825758884)
XLA Ops:
  0.0 95.2 %shard_map.55 = bf16[256,1024]{1,0:T(8,128)(2,1)} custom-call(bf16[256,2048]{1,0:T(8,128)(2,1)} %q_ref.1, bf16[256,512]{1,0:T(8,128)(2,1)} %kv_ref.1, bf16[2048,256]{1,0:T(8,128)(2,1)} %w_ref.1, s32[2,128]{1,0:T(2,128)} %bitcast.1, s32[8]{0:T(128)} %len_ref.1), custom_call_target="tpu_custom_call" | custom-call | flops 7000000000 | bytes 4000000 | tf_op jit(solution)/shard_map/pallas_call | solution.py:428
  95.2 1.9 %copy.7 = bf16[256,1024]{1,0:T(8,128)(2,1)} copy(bf16[256,1024]{1,0:T(8,128)(2,1)} %shard_map.55) | data formatting | bytes 1048576

commit v4 on v3

--- a/solution.py
+++ b/solution.py
@@ -20,7 +20,7 @@
 NC = 16
 NT = 4
 UP, DOWN = 3, 5
-SHARED = 704
+SHARED = 608
 BOTH = 2 * GW - 2 * SHARED
 
 
@@ -30,8 +30,8 @@
 
 def kernel(
     q_ref, kv_ref, w_ref, meta_ref, len_ref, out_ref,
-    qbuf, kvb, vo, bias, hbuf, wbuf, pbuf, rbuf, sbuf, gbuf, sel, take, mbuf, msm,
-    loc, m_s, m_r, q_s, q_r, kv_s, kv_r, w_s, w_r, h_s, h_r, y_s, y_r, g_s, g_r,
+    qbuf, kvb, vo, bias, hbuf, wbuf, pbuf, rbuf, xsend, xrecv, sbuf, gbuf, sel, take, mbuf, msm,
+    loc, m_s, m_r, q_s, q_r, kv_s, kv_r, w_s, w_r, h_s, h_r, y_s, y_r, x_s, x_r, g_s, g_r,
 ):
     x = lax.axis_index("dp")
     c = lax.axis_index("ctx")
@@ -59,10 +59,9 @@
     lax.fori_loop(1, NC, greet_ctx, 0)
     for i in range(1, NT):
         pl.semaphore_signal(barrier, inc=1, device_id={"tp": lax.rem(t + i, NT)}, device_id_type=MESH)
-    for i in range(NT):
-        pl.semaphore_signal(barrier, inc=1, device_id={"dp": xq, "tp": lax.rem(t + i, NT)}, device_id_type=MESH)
+    pl.semaphore_signal(barrier, inc=1, device_id={"dp": xq}, device_id_type=MESH)
     pl.semaphore_signal(barrier, inc=1, device_id={"dp": xs}, device_id_type=MESH)
-    pl.semaphore_wait(barrier, NC - 1 + NT - 1 + NT + 1)
+    pl.semaphore_wait(barrier, NC - 1 + NT - 1 + 2)
 
     def kv_copy(i):
         if i == 0:
@@ -208,19 +207,19 @@
         return pl.ds(mult(kk * GW + j * 256, 256), 256)
 
     def h_to_partner(s, j):
-        return remote(hbuf.at[s, 0, :, h_lanes(j, k)], hbuf.at[s, 1, :, h_lanes(j, k)],
+        return remote(hbuf.at[0, s, :, h_lanes(j, k)], hbuf.at[1, s, :, h_lanes(j, k)],
                       h_s.at[0, s, j], h_r.at[0, s, j], {"dp": xq})
 
     def h_to_sibling(s, j):
-        place = hbuf.at[s, 0, :, h_lanes(j, k)]
+        place = hbuf.at[0, s, :, h_lanes(j, k)]
         return remote(place, place, h_s.at[1, s, j], h_r.at[1, s, j], {"ctx": sib})
 
     def h_forward(s, j):
-        place = hbuf.at[s, 1, :, h_lanes(j, k)]
+        place = hbuf.at[1, s, :, h_lanes(j, k)]
         return remote(place, place, h_s.at[2, s, j], h_r.at[2, s, j], {"ctx": sib})
 
     def h_arrival(s, j, way):
-        place = hbuf.at[s, 1, :, h_lanes(j, k)] if way == 0 else hbuf.at[s, way - 1, :, h_lanes(j, 1 - k)]
+        place = hbuf.at[1, s, :, h_lanes(j, k)] if way == 0 else hbuf.at[way - 1, s, :, h_lanes(j, 1 - k)]
         return remote(place, place, h_s.at[way, s, j], h_r.at[way, s, j], {"ctx": sib})
 
     def attend(s, j):
@@ -236,7 +235,7 @@
             score = score * SCALE + bias[s]
             weights = jnp.exp2(score - jnp.max(score, axis=1, keepdims=True)).astype(BF)
             mixed = jnp.dot(weights, values, preferred_element_type=F32)
-            hbuf[s, 0, :, pl.ds(mult(k * GW + h * HS, HS), HS)] = (mixed[:, :HS] / mixed[:, HS:]).astype(BF)
+            hbuf[0, s, :, pl.ds(mult(k * GW + h * HS, HS), HS)] = (mixed[:, :HS] / mixed[:, HS:]).astype(BF)
         h_to_partner(s, j).start()
         h_to_sibling(s, j).start()
 
@@ -314,85 +313,132 @@
 
     lax.fori_loop(0, 8, place, 0)
 
+    def column_half(o):
+        return lax.rem(z + o, 2)
+
+    def piece(e, s):
+        return pl.ds(s * TOK, TOK) if e == 1 else pl.ds(0, 2 * TOK)
+
+    pieces = ((0, 0), (1, 0), (1, 1))
+
+    def y_copy(o, e, s, i):
+        tt = lax.rem(t + 1 + i, NT)
+        return remote(pbuf.at[o, e, tt, piece(e, s)], rbuf.at[o, e, i, piece(e, s)],
+                      y_s.at[o, e, s, i], y_r.at[o, e, s, i], {"tp": tt})
+
+    def product(o, e):
+        def one(i, _):
+            tt = lax.rem(t + 1 + i, NT)
+            columns = wbuf[tt, :, pl.ds(mult(column_half(o) * 128, 128), 128)]
+            part = jnp.dot(hbuf[e].reshape(2 * TOK, 2 * GW), columns, preferred_element_type=F32)
+            pbuf[o, e, tt] = part.astype(BF)
+
+            @pl.when(i < NT - 1)
+            def _():
+                y_copy(o, e, 0, i).start()
+
+            return 0
+
+        lax.fori_loop(0, NT, one, 0)
+        if e == 1:
+            for i in range(NT - 1):
+                y_copy(o, e, 1, i).start()
+
+    def summed(o, e, s):
+        total = pbuf[o, e, t, piece(e, s)].astype(F32)
+        for i in range(NT - 1):
+            place = rbuf.at[o, e, i, piece(e, s)]
+            remote(place, place, y_s.at[o, e, s, i], y_r.at[o, e, s, i], {"ctx": sib}).wait_recv()
+            total = total + rbuf[o, e, i, piece(e, s)].astype(F32)
+        return total.astype(BF)
+
+    def x_return(o, s):
+        return remote(xsend.at[o, s], xrecv.at[o, s], x_s.at[o, s], x_r.at[o, s], {"dp": xq})
+
+    def shards(e, s):
+        return pl.ds(s, 1) if e == 1 else pl.ds(0, 2)
+
+    def g_copy(o, e, s, i):
+        a = column_half(o)
+        return remote(sbuf.at[o, e, i, shards(e, s)], gbuf.at[k, a, e, z, shards(e, s)],
+                      g_s.at[a, e, s, i], g_r.at[a, e, s, i], {"ctx": lax.rem(c + i, NC)})
+
+    def pick(o, e, s, rows):
+        picked = jnp.dot(sel[s], rows, preferred_element_type=F32)
+        sbuf[o, e, :, s] = picked.astype(BF).reshape(NC, 32, 128)
+
+    def send_packed(o, e, s):
+        def send(i, _):
+            g_copy(o, e, s, i).start()
+            return 0
+
+        lax.fori_loop(1, NC, send, 0)
+        gbuf[k, column_half(o), e, z, shards(e, s)] = sbuf[o, e, 0, shards(e, s)]
+
+    def pack(o):
+        rows = summed(o, 0, 0)
+        for s in range(2):
+            pick(o, 0, s, rows[s * TOK : (s + 1) * TOK])
+        send_packed(o, 0, 0)
+
+    def give_back(o, s):
+        xsend[o, s] = summed(o, 1, s)
+        x_return(o, s).start()
+
+    def pack_returned(o, s):
+        x_return(o, s).wait_recv()
+        pick(o, 1, s, xrecv[o, s])
+        send_packed(o, 1, s)
+
     w_arrived(False, 4, 1)
     w_arrived(True, 2, 1)
+    for up, s in w_steps:
+        if s % 2 == 0:
+            w_shared(up, s).wait_recv()
+    for s in range(2):
+        for j in range(4):
+            h_arrival(s, j, 1).wait_recv()
     h_pass_on(0, 0)
+    product(0, 0)
     h_pass_on(0, 1)
     w_arrived(False, 5, 0)
     w_arrived(True, 3, 1)
     h_pass_on(0, 2)
     h_pass_on(0, 3)
-    for up, s in w_steps:
-        if 0 in w_parts(up, s):
-            w_shared(up, s).wait_recv()
     for s in range(2):
         for j in range(4):
-            h_arrival(s, j, 1).wait_recv()
             h_arrival(s, j, 2).wait_recv()
-
-    def y_copy(s, a, i):
-        own = i < NT - 1
-        tt = lax.rem(t + 1 + (i if own else i - NT + 1), NT)
-        where = {"tp": tt} if own else {"dp": xq, "tp": tt}
-        return remote(pbuf.at[s, tt, a, 0 if own else 1], rbuf.at[s, a, i], y_s.at[s, a, i], y_r.at[s, a, i], where)
-
-    for s in range(2):
-        for i in range(NT):
-            tt = lax.rem(t + 1 + i, NT)
-            part = jnp.dot(hbuf[s].reshape(2 * TOK, 2 * GW), wbuf[tt], preferred_element_type=F32).astype(BF)
-            for a in range(2):
-                pbuf[s, tt, a] = part[:, a * 128 : a * 128 + 128].reshape(2, TOK, 128)
-            y_copy(s, 0, NT - 1 + i).start()
-            if i < NT - 1:
-                y_copy(s, 0, i).start()
-        for i in range(NT):
-            y_copy(s, 1, NT - 1 + i).start()
-            if i < NT - 1:
-                y_copy(s, 1, i).start()
-
-    def g_copy(s, e, i):
-        return remote(sbuf.at[s, e, i], gbuf.at[k, e, 2 * z + s], g_s.at[s, e, i], g_r.at[s, e, i],
-                      {"ctx": lax.rem(c + i, NC)})
-
-    for s in range(2):
-        for e in range(2):
-            for i in range(7):
-                place = rbuf.at[s, e, i]
-                remote(place, place, y_s.at[s, e, i], y_r.at[s, e, i], {"ctx": sib}).wait_recv()
-            own = pbuf[s, t, e, 0].astype(F32)
-            for i in range(3):
-                own = own + rbuf[s, e, i].astype(F32)
-            other = rbuf[s, e, 3].astype(F32)
-            for i in range(4, 7):
-                other = other + rbuf[s, e, i].astype(F32)
-            both = jnp.concatenate([own.astype(BF), other.astype(BF)], axis=1)
-            rows = jnp.dot(sel[s], both, preferred_element_type=F32)
-            sbuf[s, e] = rows.astype(BF).reshape(NC, 32, 256)
-
-            def send(i, _):
-                g_copy(s, e, i).start()
+    product(0, 1)
+    for up, s in w_steps:
+        if s % 2 == 1 and 0 in w_parts(up, s):
+            w_shared(up, s).wait_recv()
+    pack(0)
+    give_back(0, 0)
+    product(1, 0)
+    give_back(0, 1)
+    pack_returned(0, 0)
+    product(1, 1)
+    pack_returned(0, 1)
+    pack(1)
+    give_back(1, 0)
+    give_back(1, 1)
+    pack_returned(1, 0)
+    pack_returned(1, 1)
+
+    for e in range(2):
+        for a in range(2):
+            def g_wait(i, _):
+                src = lax.rem(c + NC - i, NC)
+                for s in range(2 if e == 1 else 1):
+                    place = gbuf.at[lax.rem(src, 2), a, e, src // 2, shards(e, s)]
+                    remote(place, place, g_s.at[a, e, s, i], g_r.at[a, e, s, i], {"ctx": sib}).wait_recv()
                 return 0
 
-            lax.fori_loop(1, NC, send, 0)
-            gbuf[k, e, 2 * z + s] = sbuf[s, e, 0]
-
-    def g_wait(i, _):
-        src = lax.rem(c + NC - i, NC)
-        for s in range(2):
-            for e in range(2):
-                place = gbuf.at[lax.rem(src, 2), e, 2 * (src // 2) + s]
-                remote(place, place, g_s.at[s, e, i], g_r.at[s, e, i], {"ctx": sib}).wait_recv()
-        return 0
-
-    lax.fori_loop(1, NC, g_wait, 0)
-
-    for kk in range(2):
-        for a in range(2):
-            rows = jnp.dot(take[...], gbuf[kk, a].reshape(2 * TOK, 256), preferred_element_type=F32).astype(BF)
-            first, second = rows[:, :128], rows[:, 128:]
-            at = a * 512 + kk * 256
-            out_ref[:, at : at + 128] = jnp.where(half == 0, first, second)
-            out_ref[:, at + 128 : at + 256] = jnp.where(half == 0, second, first)
+            lax.fori_loop(1, NC, g_wait, 0)
+            for kk in range(2):
+                rows = jnp.dot(take[...], gbuf[kk, a, e].reshape(2 * TOK, 128), preferred_element_type=F32)
+                at = a * 512 + kk * 256 + (half if e == 0 else 1 - half) * 128
+                out_ref[:, pl.ds(mult(at, 128), 128)] = rows.astype(BF)
 
     for i in range(5):
         kv_copy(i).wait_send()
@@ -407,16 +453,18 @@
             h_to_partner(s, j).wait_send()
             h_to_sibling(s, j).wait_send()
             h_forward(s, j).wait_send()
-    for s in range(2):
-        for a in range(2):
-            for i in range(7):
-                y_copy(s, a, i).wait_send()
+    for o in range(2):
+        for s in range(2):
+            x_return(o, s).wait_send()
+        for e, s in pieces:
+            for i in range(NT - 1):
+                y_copy(o, e, s, i).wait_send()
 
     def sent(i, _):
         m_copy(i).wait_send()
-        for s in range(2):
-            for e in range(2):
-                g_copy(s, e, i).wait_send()
+        for o in range(2):
+            for e, s in pieces:
+                g_copy(o, e, s, i).wait_send()
         return 0
 
     lax.fori_loop(1, NC, sent, 0)
@@ -437,10 +485,12 @@
             pltpu.VMEM((2, TOK, NK), F32),
             pltpu.VMEM((2, 2, TOK, 2 * GW), BF),
             pltpu.VMEM((NT, 2 * GW, 256), BF),
-            pltpu.VMEM((2, NT, 2, 2, TOK, 128), BF),
-            pltpu.VMEM((2, 2, 7, TOK, 128), BF),
-            pltpu.VMEM((2, 2, NC, 32, 256), BF),
-            pltpu.VMEM((2, 2, NC, 32, 256), BF),
+            pltpu.VMEM((2, 2, NT, 2 * TOK, 128), BF),
+            pltpu.VMEM((2, 2, NT - 1, 2 * TOK, 128), BF),
+            pltpu.VMEM((2, 2, TOK, 128), BF),
+            pltpu.VMEM((2, 2, TOK, 128), BF),
+            pltpu.VMEM((2, 2, NC, 2, 32, 128), BF),
+            pltpu.VMEM((2, 2, 2, NZ, 2, 32, 128), BF),
             pltpu.VMEM((2, 512, TOK), BF),
             pltpu.VMEM((TOK, 512), BF),
             pltpu.VMEM((NC, 2, 128), jnp.int32),
@@ -451,8 +501,9 @@
             dma((5,)), dma((6,)),
             dma((8, 3)), dma((8, 3)),
             dma((3, 2, 4)), dma((3, 2, 4)),
-            dma((2, 2, 7)), dma((2, 2, 7)),
-            dma((2, 2, NC)), dma((2, 2, NC)),
+            dma((2, 2, 2, 3)), dma((2, 2, 2, 3)),
+            dma((2, 2)), dma((2, 2)),
+            dma((2, 2, 2, NC)), dma((2, 2, 2, NC)),
         ],
         compiler_params=pltpu.CompilerParams(
             collective_id=0, has_side_effects=True, vmem_limit_bytes=56 * 1024 * 1024

time: 98.2 us -> 95.5 us (0.973); the launches traced: 97 us -> 95.3 us
  Pallas kernels: 95.2 us -> 93.4 us
    pallas_call x1, Pallas kernels: 95.2 us -> 93.4 us  [local(): pl.pallas_call(kernel, out_shape=jax.ShapeDtypeStruct((TOK, 1024), BF), i...]
where the time goes in v4:
time: 95.5 us; the launch traced here: 95.3 us
  Pallas kernels  93.4 us (98%)
  local copies, waits for them, and re-layouts  1.87 us (2%)
    pallas_call x1, Pallas kernels, local(): pl.pallas_call(kernel, out_shape=jax.ShapeDtypeStruct((TOK, 1024), BF), i...  93.4 us

profile of v4, /device:TPU:1, one launch (start us, length us, event | category | flops | bytes accessed | tf_op | source)
XLA Modules:
  0.0 95.3 jit_solution(8983318440367451980)
XLA Ops:
  0.0 93.4 %shard_map.55 = bf16[256,1024]{1,0:T(8,128)(2,1)} custom-call(bf16[256,2048]{1,0:T(8,128)(2,1)} %q_ref.1, bf16[256,512]{1,0:T(8,128)(2,1)} %kv_ref.1, bf16[2048,256]{1,0:T(8,128)(2,1)} %w_ref.1, s32[2,128]{1,0:T(2,128)} %bitcast.1, s32[8]{0:T(128)} %len_ref.1), custom_call_target="tpu_custom_call" | custom-call | flops 7000000000 | bytes 4000000 | tf_op jit(solution)/shard_map/pallas_call | solution.py:476
  93.5 1.9 %copy.7 = bf16[256,1024]{1,0:T(8,128)(2,1)} copy(bf16[256,1024]{1,0:T(8,128)(2,1)} %shard_map.55) | data formatting | bytes 1048576

commit v5 on v4

--- a/solution.py
+++ b/solution.py
@@ -199,7 +199,6 @@
     widen(2, 4)
     w_arrived(False, 1, 0)
     w_arrived(False, 1, 1)
-    w_arrived(False, 2, 0)
     kv_arrival(1).wait_recv()
     widen(1, 1)
 
@@ -244,6 +243,7 @@
         h_forward(s, j).start()
 
     attend(1, 0)
+    w_arrived(False, 2, 0)
     w_arrived(False, 2, 1)
     attend(1, 1)
     w_arrived(True, 1, 0)
@@ -413,8 +413,8 @@
         if s % 2 == 1 and 0 in w_parts(up, s):
             w_shared(up, s).wait_recv()
     pack(0)
+    product(1, 0)
     give_back(0, 0)
-    product(1, 0)
     give_back(0, 1)
     pack_returned(0, 0)
     product(1, 1)
@@ -424,21 +424,6 @@
     give_back(1, 1)
     pack_returned(1, 0)
     pack_returned(1, 1)
-
-    for e in range(2):
-        for a in range(2):
-            def g_wait(i, _):
-                src = lax.rem(c + NC - i, NC)
-                for s in range(2 if e == 1 else 1):
-                    place = gbuf.at[lax.rem(src, 2), a, e, src // 2, shards(e, s)]
-                    remote(place, place, g_s.at[a, e, s, i], g_r.at[a, e, s, i], {"ctx": sib}).wait_recv()
-                return 0
-
-            lax.fori_loop(1, NC, g_wait, 0)
-            for kk in range(2):
-                rows = jnp.dot(take[...], gbuf[kk, a, e].reshape(2 * TOK, 128), preferred_element_type=F32)
-                at = a * 512 + kk * 256 + (half if e == 0 else 1 - half) * 128
-                out_ref[:, pl.ds(mult(at, 128), 128)] = rows.astype(BF)
 
     for i in range(5):
         kv_copy(i).wait_send()
@@ -462,12 +447,33 @@
 
     def sent(i, _):
         m_copy(i).wait_send()
-        for o in range(2):
-            for e, s in pieces:
-                g_copy(o, e, s, i).wait_send()
+        for e, s in pieces:
+            g_copy(0, e, s, i).wait_send()
         return 0
 
     lax.fori_loop(1, NC, sent, 0)
+
+    for e in range(2):
+        for a in range(2):
+            def g_wait(i, _):
+                src = lax.rem(c + NC - i, NC)
+                for s in range(2 if e == 1 else 1):
+                    place = gbuf.at[lax.rem(src, 2), a, e, src // 2, shards(e, s)]
+                    remote(place, place, g_s.at[a, e, s, i], g_r.at[a, e, s, i], {"ctx": sib}).wait_recv()
+                return 0
+
+            lax.fori_loop(1, NC, g_wait, 0)
+            for kk in range(2):
+                rows = jnp.dot(take[...], gbuf[kk, a, e].reshape(2 * TOK, 128), preferred_element_type=F32)
+                at = a * 512 + kk * 256 + (half if e == 0 else 1 - half) * 128
+                out_ref[:, pl.ds(mult(at, 128), 128)] = rows.astype(BF)
+
+    def sent_last(i, _):
+        for e, s in pieces:
+            g_copy(1, e, s, i).wait_send()
+        return 0
+
+    lax.fori_loop(1, NC, sent_last, 0)
 
 
 def local(queries, key_value_vectors, out_weight, doc_lengths, shard_of):

time: 95.5 us -> 93.8 us (0.982)
  Pallas kernels: 93.4 us -> 91.8 us
    pallas_call x1, Pallas kernels: 93.4 us -> 91.8 us  [local(): pl.pallas_call(kernel, out_shape=jax.ShapeDtypeStruct((TOK, 1024), BF), i...]
where the time goes in v5:
time: 93.8 us; the launch traced here: 93.6 us
  Pallas kernels  91.8 us (98%)
  local copies, waits for them, and re-layouts  1.87 us (2%)
    pallas_call x1, Pallas kernels, local(): pl.pallas_call(kernel, out_shape=jax.ShapeDtypeStruct((TOK, 1024), BF), i...  91.8 us

profile of v5, /device:TPU:1, one launch (start us, length us, event | category | flops | bytes accessed | tf_op | source)
XLA Modules:
  0.0 93.6 jit_solution(16717121841407274229)
XLA Ops:
  0.0 91.8 %shard_map.55 = bf16[256,1024]{1,0:T(8,128)(2,1)} custom-call(bf16[256,2048]{1,0:T(8,128)(2,1)} %q_ref.1, bf16[256,512]{1,0:T(8,128)(2,1)} %kv_ref.1, bf16[2048,256]{1,0:T(8,128)(2,1)} %w_ref.1, s32[2,128]{1,0:T(2,128)} %bitcast.1, s32[8]{0:T(128)} %len_ref.1), custom_call_target="tpu_custom_call" | custom-call | flops 7000000000 | bytes 4000000 | tf_op jit(solution)/shard_map/pallas_call | solution.py:482
  91.8 1.9 %copy.7 = bf16[256,1024]{1,0:T(8,128)(2,1)} copy(bf16[256,1024]{1,0:T(8,128)(2,1)} %shard_map.55) | data formatting | bytes 1048576

commit v6 on v5

--- a/solution.py
+++ b/solution.py
@@ -244,25 +244,25 @@
 
     attend(1, 0)
     w_arrived(False, 2, 0)
+    attend(1, 1)
     w_arrived(False, 2, 1)
-    attend(1, 1)
-    w_arrived(True, 1, 0)
     attend(1, 2)
     attend(1, 3)
+    w_arrived(True, 1, 0)
     w_arrived(False, 3, 0)
     kv_arrival(0).wait_recv()
     widen(0, 1)
     attend(0, 0)
     h_pass_on(1, 0)
+    attend(0, 1)
+    w_arrived(False, 3, 1)
     w_arrived(True, 1, 1)
-    w_arrived(False, 3, 1)
-    attend(0, 1)
     h_pass_on(1, 1)
     attend(0, 2)
     h_pass_on(1, 2)
+    attend(0, 3)
+    w_arrived(False, 4, 0)
     w_arrived(True, 2, 0)
-    w_arrived(False, 4, 0)
-    attend(0, 3)
     h_pass_on(1, 3)
 
     def m_wait(i, _):

time: 93.8 us -> 93.6 us (level)
  no operation moved by 1% of the time
where the time goes in v6:
time: 93.6 us; the launch traced here: 93.5 us
  Pallas kernels  91.6 us (98%)
  local copies, waits for them, and re-layouts  1.87 us (2%)
    pallas_call x1, Pallas kernels, local(): pl.pallas_call(kernel, out_shape=jax.ShapeDtypeStruct((TOK, 1024), BF), i...  91.6 us

profile of v6, /device:TPU:1, one launch (start us, length us, event | category | flops | bytes accessed | tf_op | source)
XLA Modules:
  0.0 93.5 jit_solution(3292537539629766683)
XLA Ops:
  0.0 91.6 %shard_map.55 = bf16[256,1024]{1,0:T(8,128)(2,1)} custom-call(bf16[256,2048]{1,0:T(8,128)(2,1)} %q_ref.1, bf16[256,512]{1,0:T(8,128)(2,1)} %kv_ref.1, bf16[2048,256]{1,0:T(8,128)(2,1)} %w_ref.1, s32[2,128]{1,0:T(2,128)} %bitcast.1, s32[8]{0:T(128)} %len_ref.1), custom_call_target="tpu_custom_call" | custom-call | flops 7000000000 | bytes 4000000 | tf_op jit(solution)/shard_map/pallas_call | solution.py:482
  91.6 1.9 %copy.7 = bf16[256,1024]{1,0:T(8,128)(2,1)} copy(bf16[256,1024]{1,0:T(8,128)(2,1)} %shard_map.55) | data formatting | bytes 1048576
